TPU v7x, 32 devices: a whole 2x2x4 slice. The times are simulated.
32 devices in a mesh: seq: 2 (over y), ctx: 4 (over x, core), fsdp: 4 (over z).
Axes of the slice: x: 2, y: 2, z: 4, core: 2. Of those that a mesh axis runs over, the one named last changes fastest.
Arguments:
- inputs: bfloat16 [16, 1024, 768], P(('seq', 'fsdp'), 'ctx'), may hold values from -6 to 6
- positions: int32 [16, 1024], P(('seq', 'fsdp')), may hold values from 0 to 1534, as said below
- w_query: bfloat16 [768, 768], P('fsdp'), may hold values from -0.109375 to 0.109375
- w_key: bfloat16 [768, 768], P('fsdp'), may hold values from -0.109375 to 0.109375
- w_value: bfloat16 [768, 768], P('fsdp'), may hold values from -0.21875 to 0.21875
- w_output: bfloat16 [768, 768], P(None, 'fsdp'), may hold values from -1.75 to 1.75
- gain_attn: bfloat16 [768], P('fsdp'), may hold values from 0.099609375 to 1.8984375
- rel_table: bfloat16 [32, 12], P('fsdp'), may hold values from -4 to 4
- w_in: bfloat16 [768, 3072], P('fsdp'), may hold values from -0.21875 to 0.21875
- w_out: bfloat16 [3072, 768], P(None, 'fsdp'), may hold values from -0.109375 to 0.109375
- gain_ffn: bfloat16 [768], P('fsdp'), may hold values from 0.099609375 to 1.8984375
- cotangent: bfloat16 [16, 1024, 768], P(('seq', 'fsdp'), 'ctx'), may hold values from -6 to 6
Outputs:
- output: bfloat16 [16, 1024, 768], P(('seq', 'fsdp'), 'ctx')
- input_grad: float32 [16, 1024, 768], P(('seq', 'fsdp'), 'ctx')
- grad_w_query: float32 [768, 768], P('fsdp')
- grad_w_key: float32 [768, 768], P('fsdp')
- grad_w_value: float32 [768, 768], P('fsdp')
- grad_w_output: float32 [768, 768], P(None, 'fsdp')
- grad_gain_attn: float32 [768], P('fsdp')
- grad_rel_table: float32 [32, 12], P('fsdp')
- grad_w_in: float32 [768, 3072], P('fsdp')
- grad_w_out: float32 [3072, 768], P(None, 'fsdp')
- grad_gain_ffn: float32 [768], P('fsdp')
Inputs may be any that keep to these rules, and one draw needn't show every extreme that they name: In each sequence the first position is 0, positions rise by 1 or 2 from one token to the next, and the last position of every sequence is exactly 1534.
All inputs are finite; a program needn't handle non-finite values.
Results may differ from a plain program's by a relative error of at most 0.023.
Values may be sent and summed in bfloat16 or wider, within the bound.
A program may use at most 192 MiB of HBM per device.

v0:
```python
import functools
import math

import jax
import jax.numpy as jnp
from jax import lax
from jax.experimental import pallas as pl
from jax.experimental.pallas import tpu as pltpu
from jax.sharding import PartitionSpec as P

MESH = pl.DeviceIdType.MESH
F32 = jnp.float32
BF = jnp.bfloat16
EPS = 1e-06
BORDERS = (12, 16, 23, 32, 46, 64, 91)
LOG2E = math.log2(math.e)
T = 128


def dot_nn(a, b):
    return jnp.dot(a, b, preferred_element_type=F32)


def dot_nt(a, b):
    return lax.dot_general(a, b, (((1,), (1,)), ((), ())), preferred_element_type=F32)


def dot_tn(a, b):
    return lax.dot_general(a, b, (((0,), (0,)), ((), ())), preferred_element_type=F32)


def bucket_of(offset):
    magnitude = jnp.abs(offset)
    logbins = jnp.full_like(magnitude, 8)
    for border in BORDERS:
        logbins = logbins + jnp.where(magnitude >= border, 1, 0)
    return jnp.where(magnitude < 8, magnitude, logbins) + jnp.where(offset > 0, 16, 0)


def pick(values, index):
    return jnp.take_along_axis(values, index, axis=1, mode="promise_in_bounds")


class Place:
    def __init__(self, z_count):
        self.y = lax.axis_index("seq")
        self.ctx = lax.axis_index("ctx")
        self.z = lax.axis_index("fsdp")
        self.x = self.ctx // 2
        self.core = self.ctx % 2
        self.col = self.y * 2 + self.x
        self.z_count = z_count
        self.sib = (self.y, self.x * 2 + 1 - self.core, self.z)
        self.xn = (self.y, (1 - self.x) * 2 + self.core, self.z)
        self.yn = (1 - self.y, self.ctx, self.z)

    def zn(self, d):
        return (self.y, self.ctx, lax.rem(self.z + d, self.z_count))


def remote(src, dst, send, recv, device):
    return pltpu.make_async_remote_copy(
        src_ref=src, dst_ref=dst, send_sem=send, recv_sem=recv, device_id=device, device_id_type=MESH
    )


class Gather:
    def __init__(self, w, ssem, rsem, slot, lo, mid, hi, here, shard):
        self.w, self.ssem, self.rsem, self.slot = w, ssem, rsem, slot
        self.lo, self.mid, self.hi = lo, mid, hi
        self.here, self.shard, self.piece = here, shard, shard // 4

    def view(self, z, col, lo, hi):
        if self.mid is None:
            return self.w.at[pl.ds(pl.multiple_of(z * self.shard, 16), self.shard), pl.ds(lo, hi - lo)]
        first = pl.multiple_of(z * self.shard + col * self.piece, 16)
        return self.w.at[pl.ds(first, self.piece), pl.ds(lo, hi - lo)]

    def copy(self, kind, d, arriving):
        p = self.here
        zs = lax.rem(p.z + p.z_count - d, p.z_count)
        col_x, col_y, col_d = p.y * 2 + 1 - p.x, (1 - p.y) * 2 + p.x, (1 - p.y) * 2 + 1 - p.x
        index = kind * 3 + d - 1
        send, recv = self.ssem.at[self.slot, index], self.rsem.at[self.slot, index]
        if kind == 0:
            ref = self.view(zs if arriving else p.z, p.col, self.lo, self.hi)
            return remote(ref, ref, send, recv, p.zn(d))
        if kind == 1:
            ref = self.view(zs, col_x if arriving else p.col, self.lo, self.hi)
            return remote(ref, ref, send, recv, p.xn)
        if kind == 2:
            ref = self.view(zs, col_y if arriving else p.col, self.lo, self.hi)
            return remote(ref, ref, send, recv, p.yn)
        if kind == 3:
            ref = self.view(zs, col_d if arriving else col_x, self.lo, self.mid)
            return remote(ref, ref, send, recv, p.yn)
        ref = self.view(zs, col_d if arriving else col_y, self.mid, self.hi)
        return remote(ref, ref, send, recv, p.xn)

    def start(self):
        for d in (1, 3, 2):
            self.copy(0, d, False).start()

    def pass_z(self):
        for d in (1, 3, 2):
            self.copy(0, d, True).wait_recv()
            self.copy(1, d, False).start()
            self.copy(2, d, False).start()

    def pass_plane(self):
        for d in (1, 3, 2):
            self.copy(1, d, True).wait_recv()
            self.copy(3, d, False).start()
            self.copy(2, d, True).wait_recv()
            self.copy(4, d, False).start()

    def finish(self):
        for d in (1, 3, 2):
            if self.mid is None:
                self.copy(0, d, True).wait_recv()
            else:
                self.copy(3, d, True).wait_recv()
                self.copy(4, d, True).wait_recv()

    def drain(self):
        for kind in range(1 if self.mid is None else 5):
            for d in (1, 3, 2):
                self.copy(kind, d, False).wait_send()


class Swap:
    def __init__(self, source, whole, ssem, rsem, lsem, here, rows):
        self.source, self.whole, self.ssem, self.rsem, self.lsem = source, whole, ssem, rsem, lsem
        self.here, self.rows = here, rows

    def block(self, ctx):
        return self.whole.at[pl.ds(pl.multiple_of(ctx * self.rows, 16), self.rows)]

    def own(self):
        return pltpu.make_async_copy(self.source.at[self.here.x], self.block(self.here.ctx), self.lsem)

    def over(self, arriving):
        p = self.here
        ctx = (1 - p.x) * 2 + p.core if arriving else p.ctx
        return remote(self.source.at[1 - p.x], self.block(ctx), self.ssem.at[0], self.rsem.at[0], p.xn)

    def pair(self, arriving):
        p = self.here
        ctx = p.x * 2 + 1 - p.core if arriving else p.ctx
        return remote(self.source.at[p.x], self.block(ctx), self.ssem.at[1], self.rsem.at[1], p.sib)

    def forward(self, arriving):
        p = self.here
        ctx = (1 - p.x) * 2 + (1 - p.core if arriving else p.core)
        return remote(self.block(ctx), self.block(ctx), self.ssem.at[2], self.rsem.at[2], p.sib)

    def start(self):
        self.over(False).start()
        self.own().start()
        self.pair(False).start()

    def relay(self):
        self.over(True).wait_recv()
        self.forward(False).start()

    def finish(self):
        self.own().wait()
        self.pair(True).wait_recv()
        self.forward(True).wait_recv()

    def drain(self):
        self.over(False).wait_send()
        self.pair(False).wait_send()
        self.forward(False).wait_send()


def enter(partners):
    barrier = pltpu.get_barrier_semaphore()
    for partner in partners:
        pl.semaphore_signal(barrier, inc=1, device_id=partner, device_id_type=MESH)
    pl.semaphore_wait(barrier, len(partners))


class Reduce:
    def __init__(self, g, r1, r2, r3, r1z, r2z, rz, fin, gfin, ssem, rsem, lsem, here, z_first):
        self.g, self.r3, self.rz, self.fin, self.gfin = g, r3, rz, fin, gfin
        self.ones, self.twos = (r1z, r1), (r2z, r2)
        self.ssem, self.rsem, self.lsem, self.here, self.z_first = ssem, rsem, lsem, here, z_first
        self.width = g.shape[-1]
        self.lo = pl.ds(0, self.width // 2)
        self.hi = pl.ds(self.width // 2, self.width // 2)
        self.piece = g.shape[4]

    def rows_z(self, c):
        return pl.ds(self.here.z, 1) if c < self.z_first else pl.ds(0, self.here.z_count)

    def count(self, c):
        return 1 if c < self.z_first else self.here.z_count

    def r1(self, c):
        return self.ones[0].at[c] if c < self.z_first else self.ones[1].at[c - self.z_first]

    def r2(self, c):
        return self.twos[0].at[c] if c < self.z_first else self.twos[1].at[c - self.z_first]

    def link(self, c, index, src, dst, device):
        return remote(src, dst, self.ssem.at[c, index], self.rsem.at[c, index], device)

    def x1(self, c):
        p = self.here
        return self.link(c, 0, self.g.at[c, 1 - p.x, :, self.rows_z(c), :, self.lo], self.r1(c).at[0], p.xn)

    def y1(self, c):
        p = self.here
        return self.link(c, 1, self.g.at[c, :, 1 - p.y, self.rows_z(c), :, self.hi], self.r1(c).at[1], p.yn)

    def x2(self, c):
        p = self.here
        return self.link(c, 2, self.g.at[c, p.x, 1 - p.y, self.rows_z(c), :, self.lo], self.r2(c).at[0], p.yn)

    def y2(self, c):
        p = self.here
        return self.link(c, 3, self.g.at[c, 1 - p.x, p.y, self.rows_z(c), :, self.hi], self.r2(c).at[1], p.xn)

    def z1(self, c, d):
        p = self.here
        to = lax.rem(p.z + d, p.z_count)
        if c < self.z_first:
            return self.link(c, 3 + d, self.g.at[c, :, :, to], self.rz.at[c, d - 1], p.zn(d))
        return self.link(c, 3 + d, self.g.at[c, p.x, p.y, to], self.r3.at[c - self.z_first, d - 1], p.zn(d))

    def over_x(self, c, arriving):
        p = self.here
        col = p.y * 2 + 1 - p.x if arriving else p.col
        return self.link(c, 7, self.fin.at[c], self.gfin.at[p.core, c, col], p.xn)

    def over_y(self, c, arriving):
        p = self.here
        ref = self.gfin.at[p.core, c, pl.ds((1 - p.y if arriving else p.y) * 2, 2)]
        return self.link(c, 8, ref, ref, p.yn)

    def keep(self, c):
        return pltpu.make_async_copy(self.fin.at[c], self.gfin.at[self.here.core, c, self.here.col], self.lsem.at[c])

    def pair(self, c, arriving):
        core = 1 - self.here.core if arriving else self.here.core
        return self.link(c, 9, self.gfin.at[core, c], self.gfin.at[core, c], self.here.sib)

    def start(self, c):
        if c < self.z_first:
            for d in (1, 3, 2):
                self.z1(c, d).start()
        else:
            self.plane(c)

    def gathered_z(self, c):
        p = self.here
        for d in (1, 3, 2):
            self.z1(c, d).wait_recv()
        for x in range(2):
            for y in range(2):
                total = self.g[c, x, y, p.z].astype(F32)
                for d in range(3):
                    total = total + self.rz[c, d, x, y].astype(F32)
                self.g[c, x, y, p.z] = total.astype(BF)
        self.plane(c)

    def plane(self, c):
        self.x1(c).start()
        self.y1(c).start()

    def second(self, c):
        p = self.here
        h = self.width // 2

        def zi(k):
            return p.z if c < self.z_first else k

        self.x1(c).wait_recv()

        def add_x(k, carry):
            for y in range(2):
                self.g[c, p.x, y, zi(k), :, :h] = (
                    self.g[c, p.x, y, zi(k), :, :h].astype(F32) + self.r1(c)[0, y, k].astype(F32)
                ).astype(BF)
            return carry

        lax.fori_loop(0, self.count(c), add_x, 0)
        self.x2(c).start()
        self.y1(c).wait_recv()

        def add_y(k, carry):
            for x in range(2):
                self.g[c, x, p.y, zi(k), :, h:] = (
                    self.g[c, x, p.y, zi(k), :, h:].astype(F32) + self.r1(c)[1, x, k].astype(F32)
                ).astype(BF)
            return carry

        lax.fori_loop(0, self.count(c), add_y, 0)
        self.y2(c).start()

    def third(self, c):
        p = self.here
        h = self.width // 2
        self.x2(c).wait_recv()
        self.y2(c).wait_recv()
        if c < self.z_first:
            self.fin[c, :, :h] = (self.g[c, p.x, p.y, p.z, :, :h].astype(F32) + self.r2(c)[0, 0].astype(F32)).astype(BF)
            self.fin[c, :, h:] = (self.g[c, p.x, p.y, p.z, :, h:].astype(F32) + self.r2(c)[1, 0].astype(F32)).astype(BF)
            self.publish(c)
            return

        def add(k, carry):
            self.g[c, p.x, p.y, k, :, :h] = (
                self.g[c, p.x, p.y, k, :, :h].astype(F32) + self.r2(c)[0, k].astype(F32)
            ).astype(BF)
            self.g[c, p.x, p.y, k, :, h:] = (
                self.g[c, p.x, p.y, k, :, h:].astype(F32) + self.r2(c)[1, k].astype(F32)
            ).astype(BF)
            return carry

        lax.fori_loop(0, p.z_count, add, 0)
        for d in (1, 3, 2):
            self.z1(c, d).start()

    def fourth(self, c):
        if c < self.z_first:
            return
        p = self.here
        for d in (1, 3, 2):
            self.z1(c, d).wait_recv()
        total = self.g[c, p.x, p.y, p.z].astype(F32)
        for d in range(3):
            total = total + self.r3[c - self.z_first, d].astype(F32)
        self.fin[c] = total.astype(BF)
        self.publish(c)

    def publish(self, c):
        self.over_x(c, False).start()
        self.keep(c).start()

    def fifth(self, c):
        self.over_x(c, True).wait_recv()
        self.keep(c).wait()
        self.over_y(c, False).start()

    def sixth(self, c):
        self.over_y(c, True).wait_recv()
        self.pair(c, False).start()

    def last(self, c):
        self.pair(c, True).wait_recv()
        for copy in (self.x1(c), self.y1(c), self.x2(c), self.y2(c), self.over_x(c, False), self.over_y(c, False), self.pair(c, False)):
            copy.wait_send()
        for d in (1, 3, 2):
            self.z1(c, d).wait_send()


def edges():
    starts, buckets = [], [15]
    lows = (8,) + BORDERS
    for b in range(14, 7, -1):
        starts.append(1 - lows[b - 7])
        buckets.append(b)
    for n in range(7, -1, -1):
        starts.append(-n)
        buckets.append(n)
    for n in range(1, 8):
        starts.append(n)
        buckets.append(16 + n)
    for b in range(8, 16):
        starts.append(lows[b - 8])
        buckets.append(16 + b)
    return starts, buckets


def gelu_parts(v):
    c0 = math.sqrt(2.0 / math.pi)
    sq = v * v
    th = jnp.tanh(v * (c0 + (c0 * 0.044715) * sq))
    half = 0.5 + 0.5 * th
    slope = half + (0.5 * v) * (1.0 - th * th) * (c0 + (3.0 * 0.044715 * c0) * sq)
    return v * half, slope


def layer_kernel(
    inputs, positions, wq, wk, wv, wo_t, win, wout_t, extra_in, cotangent,
    out_ref, igrad_ref, gfin, evec_out, probs_out,
    w, x_all, cot_all, extra, n_t, turned, q, k, v, mixed, linv, table, pool, bound, ka, va, p_slot,
    y_in, t_in, o_send, o_in, slope, gmid, dk_acc, dv_acc, cat, stage, ig_in,
    hist, far_sum, gain_acc, e_src, e_in,
    g, r1, r2, r3, r1z, r2z, rz, fin,
    ssem, rsem, swap_s, swap_r, cot_s, cot_r, e_s, e_r, lsem, psem, y_s, y_r, t_s, t_r, o_s, o_r, out_s, out_r, u_s, u_r, ev_s, ev_r,
    g_s, g_r, g_l, osem,
):
    here = Place(lax.axis_size("fsdp"))
    p = here
    D, INNER = w.shape[0], wo_t.shape[1]
    half = INNER // 2
    ffh = win.shape[1] // 2
    shard = wq.shape[0]
    piece = shard // 4
    R = x_all.shape[0]
    heads = half // 64
    nt = R // T
    active = pool.at[:, pl.ds(0, ffh)]
    y_own = pool.at[:, pl.ds(ffh, D)]
    t_own = stage
    own_rows = pl.ds(pl.multiple_of(p.z * shard, 16), shard)
    half_cols = pl.ds(pl.multiple_of(p.core * half, 128), half)
    ff_cols = pl.ds(pl.multiple_of(p.core * ffh, 128), ffh)
    c_o, c_in, c_out, c_end = 3 * half, 4 * half, 4 * half + ffh, 4 * half + 2 * ffh

    loads = [
        pltpu.make_async_copy(wq.at[:, half_cols], w.at[own_rows, pl.ds(0, half)], lsem.at[0]),
        pltpu.make_async_copy(wk.at[:, half_cols], w.at[own_rows, pl.ds(half, half)], lsem.at[1]),
        pltpu.make_async_copy(wv.at[:, half_cols], w.at[own_rows, pl.ds(2 * half, half)], lsem.at[2]),
        pltpu.make_async_copy(win.at[:, ff_cols], w.at[own_rows, pl.ds(c_in, ffh)], lsem.at[3]),
        pltpu.make_async_copy(wo_t.at[:, half_cols], w.at[own_rows, pl.ds(c_o, half)], lsem.at[4]),
        pltpu.make_async_copy(wout_t.at[:, ff_cols], w.at[own_rows, pl.ds(c_out, ffh)], lsem.at[5]),
        pltpu.make_async_copy(extra_in, extra.at[own_rows], lsem.at[6]),
    ]
    for load in loads:
        load.start()
    enter([p.sib, p.xn, p.yn, p.zn(1), p.zn(2), p.zn(3)])
    swap = Swap(inputs, x_all, swap_s, swap_r, lsem.at[7], here, inputs.shape[1])
    swap.start()
    cot_swap = Swap(cotangent, cot_all, cot_s, cot_r, lsem.at[8], here, inputs.shape[1])

    def extra_copy(d, arriving):
        zs = lax.rem(p.z + p.z_count - d, p.z_count) if arriving else p.z
        ref = extra.at[pl.ds(pl.multiple_of(zs * shard, 16), shard)]
        return remote(ref, ref, e_s.at[d - 1], e_r.at[d - 1], p.zn(d))

    loads[6].wait()
    for d in (1, 3, 2):
        extra_copy(d, False).start()
    tracks = [(n * half, n * half + 2 * T, (n + 1) * half) for n in range(3)] + [(c_o, c_o + 2 * T, c_in)]
    tracks += [(lo, lo + 3 * T, lo + 4 * T) for lo in range(c_in, c_end - 4 * T, 4 * T)] + [(c_end - 4 * T, None, c_end)]
    gathers = [Gather(w, ssem, rsem, n, lo, mid, hi, here, shard) for n, (lo, mid, hi) in enumerate(tracks)]
    for n in range(3):
        loads[n].wait()
        gathers[n].start()
    for n in range(3, 6):
        loads[n].wait()
    for gather in gathers[3:]:
        gather.start()

    starts, classes = edges()
    lane = lax.broadcasted_iota(jnp.int32, (1, T), 1)
    pos = positions[pl.ds(p.x, 1), :]
    band = [(a, d) for a in range(nt) for d in range(3) if 0 <= a + d - 1 < nt]
    cols = {}
    early = {
        25: [gathers[1].pass_z],
        9: [gathers[0].pass_z],
        37: [gathers[0].pass_plane],
        43: [gathers[2].pass_plane],
        42: [swap.relay],
        44: [gathers[3].pass_z, gathers[4].pass_z],
        41: [gathers[1].pass_plane],
        27: [gathers[2].pass_z],
    }

    def offsets(a, d):
        if a not in cols:
            cols[a] = jnp.broadcast_to(pos[:, a * T : (a + 1) * T], (T, T)).T
        return pos[:, (a + d - 1) * T : (a + d) * T] - cols[a]

    edge = jnp.full((1, T), -(2**20), jnp.int32)
    for j, first in enumerate(starts):
        edge = jnp.where(lane == j, first, edge)
    ranks = {}

    def ranks_of(b):
        if b not in ranks:
            offsets(b, 1)
            base = pos[:, b * T : b * T + 1]
            above = cols[b] - base
            ranks[b] = base, [
                jnp.broadcast_to(jnp.sum(jnp.where(above < lane + m * T, 1.0, 0.0), axis=0, keepdims=True), (T, T)) for m in range(2)
            ]
        return ranks[b]

    for n, (a, d) in enumerate(band):
        for step in early.get(n, ()):
            step()
        offsets(a, 1)
        base, (low, high) = ranks_of(a + d - 1)
        at = jnp.clip(cols[a] + edge - base, 0, 2 * T - 1)
        count = jnp.where(at < T, pick(low, jnp.minimum(at, T - 1)), pick(high, jnp.maximum(at - T, 0)))
        bound[a * T : (a + 1) * T, d * T : (d + 1) * T] = count.astype(jnp.int32) - 1

    for d in (1, 3, 2):
        extra_copy(d, True).wait_recv()
    buckets_per = 8
    rows = [extra[zs * shard : zs * shard + 16, :].astype(F32)[:buckets_per] for zs in range(4)]
    flat = jnp.concatenate(rows + [jnp.zeros((T - 32, T), F32)], axis=0)
    table[...] = flat.T
    gains = jnp.concatenate(
        [extra[t * T : (t + 1) * T, :].astype(F32).T[0:8] for t in range(D // T)], axis=1
    )
    gain_one, gain_two = gains[0:1], gains[1:2]
    for n, (a, d) in enumerate(band):
        for step in early.get(len(band) + n, ()):
            step()
        idx = bucket_of(offsets(a, d))
        for h in range(heads):
            tab = jnp.broadcast_to(table[pl.ds(2 + p.core * heads + h, 1), :], (T, T))
            pool[a * T : (a + 1) * T, (h * 3 + d) * T : (h * 3 + d + 1) * T] = pick(tab, idx).astype(BF)
    for step in early.get(2 * len(band), ()):
        step()

    swap.finish()
    for c in range(4):
        rows = slice(c * (R // 4), (c + 1) * (R // 4))
        xf = x_all[rows, :].astype(F32)
        scale = lax.rsqrt(jnp.mean(xf * xf, axis=1, keepdims=True) + EPS)
        stage[rows, :] = (xf * scale * gain_one).astype(BF)
        n_t[:, rows] = (xf * scale * gain_one).T.astype(BF)
    for gather in gathers[:3]:
        gather.finish()

    def project(c, carry):
        rows = pl.ds(pl.multiple_of(c * 256, 256), 256)
        for n, dest in enumerate((q, k, v)):
            out = dot_nn(stage[rows, :], w[:, n * half : (n + 1) * half]).astype(BF)
            for pair in range(half // T):
                dest[pair, rows, :] = out[:, pair * T : (pair + 1) * T]
        return carry

    lax.fori_loop(0, R // 256, project, 0)

    QT = 256
    sub = QT // T
    units = R // QT
    ahead = {
        1: [gathers[5].pass_z],
        3: [gathers[6].pass_z],
        5: [gathers[4].pass_plane],
        13: [gathers[8].pass_z],
        4: [gathers[3].pass_plane, gathers[5].pass_plane],
        6: [gathers[6].pass_plane, cot_swap.start],
        9: [gathers[7].pass_z],
    }
    for step in ahead.get(-1, ()):
        step()

    def halves(h, lanes):
        return ((lanes < 64), lanes - 64) if h == 0 else ((lanes >= 64), lanes)

    def pair_step(hp, carry):
        lane_k = lax.broadcasted_iota(jnp.int32, (R, T), 1)
        tile_k = lax.broadcasted_iota(jnp.int32, (R, T), 0) // T
        for h in range(2):
            tab = table[pl.ds(2 + p.core * heads + hp * 2 + h, 1), :]
            inside, other = halves(h, lane_k)
            far = jnp.where(tile_k < other - 1, tab[:, 15:16], jnp.where(tile_k > other + 1, tab[:, 31:32], 0.0))
            far = jnp.where(other < nt, far, 0.0)
            ka[h] = jnp.where(inside, k[hp].astype(F32), far).astype(BF)
            va[h] = jnp.where(inside, v[hp].astype(F32), 1.0).astype(BF)
        lane_q = lax.broadcasted_iota(jnp.int32, (QT, T), 1)
        tile_q = lax.broadcasted_iota(jnp.int32, (QT, T), 0) // T
        for qi in range(units):
            for trip in range(heads // 2):
                if trip * units + qi in ahead:
                    pl.when(hp == trip)(lambda todo=ahead[trip * units + qi]: [step() for step in todo] and None)
            store = pltpu.make_async_copy(p_slot.at[qi % 2], probs_out.at[hp, :, pl.ds(qi * QT, QT)], psem.at[qi % 2])
            if qi < 2:
                pl.when(hp > 0)(store.wait)
            else:
                store.wait()
            rows = slice(qi * QT, (qi + 1) * QT)
            scores = []
            for h in range(2):
                inside, other = halves(h, lane_q)
                hot = jnp.where(other == tile_q + qi * sub, 1.0, 0.0)
                qm = jnp.where(inside, q[hp, rows, :].astype(F32), hot).astype(BF)
                scores.append(dot_nt(qm, ka[h]))
            mixes = []
            for h in range(2):
                strips = []
                for si in range(sub):
                    a = qi * sub + si
                    st = scores[h][si * T : (si + 1) * T]
                    lo, hi = max(a - 1, 0), min(a + 2, nt)
                    parts = [st[:, : lo * T]] if lo > 0 else []
                    lanes = pl.ds(pl.multiple_of((hp * 2 + h) * 3 * T + (lo - a + 1) * T, T), (hi - lo) * T)
                    near = pool[a * T : (a + 1) * T, lanes]
                    parts.append(st[:, lo * T : hi * T] + near.astype(F32))
                    if hi < nt:
                        parts.append(st[:, hi * T :])
                    strips.append(jnp.concatenate(parts, axis=1))
                sc = jnp.concatenate(strips, axis=0)
                m = jnp.max(sc, axis=1, keepdims=True)
                pb = jnp.exp2((sc - m) * LOG2E).astype(BF)
                p_slot[qi % 2, h] = pb
                mixes.append(dot_nn(pb, va[h]))
            store.start()
            o = jnp.where(lane < 64, mixes[0], mixes[1])
            total = pltpu.roll(jnp.where(lane < 64, mixes[1], mixes[0]), 64, 1)
            inv = 1.0 / total
            mixed[hp, rows, :] = (o * inv).astype(BF)
            linv[hp, rows, :] = inv
        return carry

    lax.fori_loop(0, heads // 2, pair_step, 0)
    for slot in range(2):
        pltpu.make_async_copy(p_slot.at[slot], probs_out.at[0, :, pl.ds(0, QT)], psem.at[slot]).wait()

    B = 256
    blocks = R // B
    FW = 512
    for step in ahead.get(3 * units, ()):
        step()
    for gather in gathers[3:7]:
        gather.finish()

    def y_copy(i, arriving=False):
        rows = pl.ds(pl.multiple_of(i * B, B), B)
        return remote(y_own.at[rows], y_in.at[rows], y_s.at[i], y_r.at[i], p.sib)

    def t_copy(i):
        rows = pl.ds(pl.multiple_of(i * B, B), B)
        return remote(t_own.at[rows], t_in.at[rows], t_s.at[i], t_r.at[i], p.sib)

    def o_copy(n):
        return remote(o_send.at[n], o_in.at[n], o_s.at[n], o_r.at[n], p.sib)

    def project_out(i, carry):
        rows = pl.ds(pl.multiple_of(i * B, B), B)
        mx = jnp.concatenate([mixed[pair, rows, :] for pair in range(half // T)], axis=1)
        y_own[rows, :] = dot_nt(mx, w[:, c_o : c_o + half]).astype(BF)
        y_copy(i).start()
        return carry

    lax.fori_loop(0, blocks, project_out, 0)
    for step in ahead.get(3 * units + 1, ()):
        step()

    def middle_of(rows):
        mid = x_all[rows, :].astype(F32) + (y_own[rows, :].astype(F32) + y_in[rows, :].astype(F32))
        return mid, lax.rsqrt(jnp.mean(mid * mid, axis=1, keepdims=True) + EPS)

    red = Reduce(g, r1, r2, r3, r1z, r2z, rz, fin, gfin, g_s, g_r, g_l, here, 2)
    between = {
        1: [gathers[7].pass_plane],
        3: [gathers[8].pass_plane],
        0: [cot_swap.relay],
    }

    def during(i, base, table):
        for n in range(blocks):
            if base + n in table:
                pl.when(i == n)(lambda todo=table[base + n]: [step() for step in todo] and None)

    def ffn_in(i, carry):
        rows = pl.ds(pl.multiple_of(i * B, B), B)
        y_copy(i).wait_recv()
        mid, scale = middle_of(rows)
        n2f = mid * scale * gain_two
        n2 = n2f.astype(BF)
        stage[rows, :] = n2
        for j in range(ffh // FW):
            hidden = dot_nn(n2, w[:, c_in + j * FW : c_in + (j + 1) * FW])
            act, slo = gelu_parts(hidden)
            active[rows, j * FW : (j + 1) * FW] = act.astype(BF)
            slope[rows, j * FW : (j + 1) * FW] = slo.astype(BF)
        during(i, 0, between)
        return carry

    lax.fori_loop(0, blocks, ffn_in, 0)
    cot_swap.finish()
    for i in range(blocks):
        rows = slice(i * B, (i + 1) * B)
        turned[:, rows] = cot_all[rows, :].astype(F32).T.astype(BF)


    def keep_pieces(c, lo, left, right):
        for n in range(0, right.shape[1], 2 * T):
            value = dot_nn(left, right[:, n : n + 2 * T])
            for zs in range(p.z_count):
                for col in range(4):
                    first_row = zs * shard + col * piece
                    g[c, col % 2, col // 2, zs, :, lo + n : lo + n + value.shape[1]] = value[first_row : first_row + piece].astype(BF)

    for c in range(ffh // FW):
        keep_pieces(c, 0, turned[...], active[:, c * FW : (c + 1) * FW])
        red.start(c)
        for step in between.get(4 + c, ()):
            step()
    for i in range(blocks):
        rows = slice(i * B, (i + 1) * B)
        turned[:, rows] = stage[rows, :].astype(F32).T.astype(BF)
    for gather in gathers[7:]:
        gather.finish()
    later = {
        2: [functools.partial(red.second, 2)],
        4: [functools.partial(red.third, 2)],
        10: [functools.partial(red.gathered_z, 0)],
    }

    def ffn_back(i, carry):
        rows = pl.ds(pl.multiple_of(i * B, B), B)
        cot = cot_all[rows, :]
        for j in range(ffh // FW):
            grad = dot_nn(cot, w[:, c_out + j * FW : c_out + (j + 1) * FW])
            cols = slice(j * FW, (j + 1) * FW)
            slope[rows, cols] = (grad * slope[rows, cols].astype(F32)).astype(BF)
        t_own[rows, :] = dot_nt(slope[rows, :], w[:, c_in:c_out]).astype(BF)
        t_copy(i).start()
        o = dot_nt(active[rows, :], w[:, c_out:c_end])
        n = i // 2

        @pl.when(i % 2 == p.core)
        def _():
            gmid[n] = o

        @pl.when(i % 2 != p.core)
        def _():
            o_send[n] = o.astype(BF)
            o_copy(n).start()

        during(i, 0, later)
        return carry

    lax.fori_loop(0, blocks, ffn_back, 0)
    for c in range(ffh // FW):
        keep_pieces(3 + c, 0, turned[...], slope[:, c * FW : (c + 1) * FW])
        for step in later.get(4 + c, ()):
            step()
        red.start(3 + c)

    gain_acc[...] = jnp.zeros_like(gain_acc)

    def back_middle(i, carry):
        rows = pl.ds(pl.multiple_of(i * B, B), B)
        t_copy(i).wait_recv()
        mid, scale = middle_of(rows)
        t = t_own[rows, :].astype(F32) + t_in[rows, :].astype(F32)
        tg = t * gain_two
        dot = jnp.mean(tg * mid, axis=1, keepdims=True)
        gm = cot_all[rows, :].astype(F32) + scale * tg - (scale * scale * scale * dot) * mid
        gy = gm.astype(BF)
        turned[:, rows] = gm.T.astype(BF)
        grad = dot_nn(gy, w[:, c_o : c_o + half])
        for pair in range(half // T):
            slope[rows, D + pair * T : D + (pair + 1) * T] = (grad[:, pair * T : (pair + 1) * T] * linv[pair, rows, :]).astype(BF)
        n = i // 2

        @pl.when(i % 2 == p.core)
        def _():
            gain_acc[1:2, :] += jnp.sum(t * mid * scale, axis=0, keepdims=True)
            o_copy(n).wait_recv()
            slope[pl.ds(pl.multiple_of(n * B, B), B), :D] = (mid + gmid[n] + o_in[n].astype(F32)).astype(BF)
            gmid[n] = gm

        during(i, 7, later)
        return carry

    lax.fori_loop(0, blocks, back_middle, 0)
    out_own = pltpu.make_async_copy(slope.at[pl.ds(pl.multiple_of(p.x * B, B), B), pl.ds(0, D)], out_ref.at[p.x], osem.at[0])
    out_over = remote(slope.at[pl.ds(pl.multiple_of((1 - p.x) * B, B), B), pl.ds(0, D)], out_ref.at[p.x], out_s.at[0], out_r.at[0], p.xn)
    out_there = remote(slope.at[pl.ds(pl.multiple_of((1 - p.x) * B, B), B), pl.ds(0, D)], out_ref.at[1 - p.x], out_s.at[0], out_r.at[0], p.xn)
    out_own.start()
    out_over.start()

    hist[...] = jnp.zeros_like(hist)
    far_sum[...] = jnp.zeros_like(far_sum)
    row_i = lax.broadcasted_iota(jnp.int32, (2 * T, 2 * T), 0)
    col_i = lax.broadcasted_iota(jnp.int32, (2 * T, 2 * T), 1)
    upto_incl = jnp.where(jnp.logical_and(row_i <= col_i, row_i // T == col_i // T), 1.0, 0.0).astype(BF)
    skip_left, skip_right = 96, 32

    def p_load(hp, qi):
        return pltpu.make_async_copy(probs_out.at[hp, :, pl.ds(qi * QT, QT)], p_slot.at[qi % 2], psem.at[qi % 2])

    p_load(0, 0).start()
    stages = {
        1: [functools.partial(red.second, 4)],
        9: [functools.partial(red.second, 5), functools.partial(red.gathered_z, 1)],
        11: [functools.partial(red.fourth, 2), functools.partial(red.second, 3), functools.partial(red.second, 7), functools.partial(red.second, 0), functools.partial(red.third, 4), functools.partial(red.second, 6)],
    }

    def lanes_of(m, hp):
        return pl.ds(pl.multiple_of(m * half + hp * T, T), T)

    def pair_back(hp, carry):
        lane_k = lax.broadcasted_iota(jnp.int32, (R, T), 1)
        tile_k = lax.broadcasted_iota(jnp.int32, (R, T), 0) // T
        for h in range(2):
            inside = (lane_k < 64) if h == 0 else (lane_k >= 64)
            other = lane_k - 64 if h == 0 else lane_k
            va[h] = jnp.where(inside, v[hp].astype(F32), jnp.where(other < 3, 1.0, 0.0)).astype(BF)
            ka[h] = jnp.where(inside, k[hp].astype(F32), jnp.where(other == tile_k, 1.0, 0.0)).astype(BF)
        dk_acc[...] = jnp.zeros_like(dk_acc)
        dv_acc[...] = jnp.zeros_like(dv_acc)
        lane_q = lax.broadcasted_iota(jnp.int32, (QT, T), 1)
        tile_q = lax.broadcasted_iota(jnp.int32, (QT, T), 0) // T
        for qi in range(units):
            for trip in range(heads // 2):
                if trip * units + qi in stages:
                    pl.when(hp == trip)(lambda todo=stages[trip * units + qi]: [step() for step in todo] and None)
            rows = slice(qi * QT, (qi + 1) * QT)
            p_load(hp, qi).wait()
            if qi + 1 < units:
                p_load(hp, qi + 1).start()
            else:
                pl.when(hp < heads // 2 - 1)(lambda: p_load(hp + 1, 0).start())
            do = slope[rows, pl.ds(pl.multiple_of(D + hp * T, T), T)].astype(F32)
            prod = do * mixed[hp, rows, :].astype(F32)
            qf = q[hp, rows, :].astype(F32)
            dps, dms, qms, dqs, grads = [], [], [], [], []
            for h in range(2):
                inside, other = halves(h, lane_q)
                rd = jnp.sum(jnp.where(inside, prod, 0.0), axis=1, keepdims=True)
                ra = rd.astype(BF).astype(F32)
                rb = (rd - ra).astype(BF).astype(F32)
                rc = rd - ra - rb
                dm = jnp.where(inside, do, 0.0)
                da = (dm - jnp.where(other == 0, ra, jnp.where(other == 1, rb, jnp.where(other == 2, rc, 0.0)))).astype(BF)
                dms.append(dm.astype(BF))
                qms.append(jnp.where(inside, qf, 0.0).astype(BF))
                dps.append(dot_nt(da, va[h]))
            for h in range(2):
                pb = p_slot[qi % 2, h]
                ds = (pb.astype(F32) * dps[h]).astype(BF)
                grads.append(ds)
                dqs.append(dot_nn(ds, ka[h]))
                dv_acc[...] += dot_tn(dms[h], pb)
                dk_acc[...] += dot_tn(qms[h], ds)
            cat[rows, lanes_of(0, hp)] = jnp.where(lane < 64, dqs[0], dqs[1]).astype(BF)
            in_tile = lax.broadcasted_iota(jnp.int32, (QT, T), 0) % T
            tile = tile_q + qi * sub
            for h in range(2):
                ds = grads[h]
                inside, other = halves(h, lane_q)
                spare = jnp.where(inside, 0.0, dqs[h])
                left = jnp.logical_or(other < tile - 1, jnp.logical_and(other == tile - 1, in_tile >= skip_left))
                right = jnp.logical_or(other > tile + 1, jnp.logical_and(other == tile + 1, in_tile < skip_right))
                for m, cond in enumerate((left, jnp.logical_and(right, other < nt), other < nt)):
                    far_sum[hp * 2 + h, m : m + 1, :] += jnp.sum(jnp.where(cond, spare, 0.0), axis=0, keepdims=True)
                found = jnp.zeros((8, T), F32)
                first_lane = min(max(qi * sub - 1, 0), nt - 4) * T
                sums_all = [dot_nn(ds[:, first_lane + m * 2 * T : first_lane + (m + 1) * 2 * T], upto_incl) for m in range(2)]
                for si in range(sub):
                    a = qi * sub + si
                    for d in range(3):
                        b = a + d - 1
                        if 0 <= b < nt:
                            r0, r1_ = (0, skip_left) if d == 0 else ((skip_right, T) if d == 2 else (0, T))
                            lane0 = b * T - first_lane
                            sums = sums_all[lane0 // (2 * T)][si * T + r0 : si * T + r1_, lane0 % (2 * T) : lane0 % (2 * T) + T]
                            idx = bound[a * T + r0 : a * T + r1_, d * T : (d + 1) * T]
                            got = jnp.where(idx >= 0, pick(sums, jnp.maximum(idx, 0)), 0.0)
                            found = found + jnp.sum(got.reshape((r1_ - r0) // 8, 8, T), axis=0)
                hist[hp * 2 + h] += found
        cat[:, lanes_of(1, hp)] = dk_acc[...].T.astype(BF)
        cat[:, lanes_of(2, hp)] = dv_acc[...].T.astype(BF)
        c = 6 + hp
        for m in range(3):
            keep_pieces(c, m * T, n_t[...], cat[:, lanes_of(m, hp)])
        keep_pieces(c, 3 * T, turned[...], mixed[hp])
        for trip in range(heads // 2):
            pl.when(hp == trip)(functools.partial(red.start, 6 + trip))
        return carry

    lax.fori_loop(0, heads // 2, pair_back, 0)

    def u_copy(n):
        return remote(slope.at[pl.ds((2 + n) * B, B), pl.ds(0, D)], o_in.at[2 + n], u_s.at[n], u_r.at[n], p.sib)

    for n in range(2):
        rows = pl.ds(pl.multiple_of((2 * n + 1 - p.core) * B, B), B)
        slope[(2 + n) * B : (3 + n) * B, :D] = dot_nt(cat[rows, :], w[:, :c_o]).astype(BF)
        u_copy(n).start()
    red.third(0)
    red.second(1)
    red.fifth(2)
    red.third(7)
    red.third(5)
    for n in range(2):
        rows = pl.ds(pl.multiple_of((2 * n + p.core) * B, B), B)
        t = dot_nt(cat[rows, :], w[:, :c_o])
        u_copy(n).wait_recv()
        t = t + o_in[2 + n].astype(F32)
        xf = x_all[rows, :].astype(F32)
        scale = lax.rsqrt(jnp.mean(xf * xf, axis=1, keepdims=True) + EPS)
        tg = t * gain_one
        dot = jnp.mean(tg * xf, axis=1, keepdims=True)
        gmid[n] = gmid[n] + scale * tg - (scale * scale * scale * dot) * xf
        gain_acc[0:1, :] += jnp.sum(t * xf * scale, axis=0, keepdims=True)
    ig_own = pltpu.make_async_copy(gmid.at[p.x], igrad_ref.at[p.x], osem.at[1])
    ig_own.start()
    slope[:B, D:] = gmid[1 - p.x].astype(BF)
    ig_over = remote(slope.at[pl.ds(0, B), pl.ds(D, D)], ig_in, out_s.at[1], out_r.at[1], p.xn)

    gains_rows = [gain_acc[m : m + 1, t * T : (t + 1) * T] for m in range(2) for t in range(D // T)]
    class_of = jnp.zeros((1, T), jnp.int32)
    for j, bkt in enumerate(classes):
        class_of = jnp.where(lane == bkt, j, class_of)
    used = jnp.logical_and(lane < 32, lane != 16)
    rows_h = []
    for h in range(heads):
        upto = jnp.sum(hist[h], axis=0, keepdims=True)
        sums = jnp.sum(far_sum[h], axis=1, keepdims=True)
        left, right, every = sums[0:1], sums[1:2], sums[2:3]
        near = every - left - right
        n_edges = len(starts)
        upto = jnp.where(lane < n_edges, upto, jnp.where(lane == n_edges, near, 0.0))
        below = jnp.where(lane == 0, 0.0, pltpu.roll(upto, 1, 1))
        per = upto - below + jnp.where(lane == 0, left, jnp.where(lane == n_edges, right, 0.0))
        rows_h.append(per)
    heads_rows = jnp.concatenate(rows_h + [jnp.zeros((8 - heads, T), F32)], axis=0)
    picked = jnp.take_along_axis(heads_rows, jnp.broadcast_to(class_of, (8, T)), axis=1)
    picked = jnp.where(used, picked, 0.0)[:heads]
    zero = jnp.zeros((heads, T), F32)
    first_half = jnp.where(p.core == 0, picked, zero)
    other_half = jnp.where(p.core == 0, zero, picked)
    e_src[0] = jnp.concatenate(gains_rows + [first_half, other_half], axis=0)

    def e_copy(n):
        device = (p.sib, p.xn, p.yn, p.zn(1), p.zn(2), p.zn(3))[n]
        return remote(e_src.at[min(n, 3)], e_in.at[n], ev_s.at[n], ev_r.at[n], device)

    red.third(6)
    ig_over.start()
    e_copy(0).start()
    e_copy(0).wait_recv()
    e_src[1] = e_src[0] + e_in[0]
    e_copy(1).start()
    red.fourth(4)
    red.fourth(5)
    red.sixth(2)
    red.fifth(0)
    red.third(3)
    red.second(8)
    e_copy(1).wait_recv()
    e_src[2] = e_src[1] + e_in[1]
    e_copy(2).start()
    red.fifth(4)
    red.fourth(6)
    e_copy(2).wait_recv()
    e_src[3] = e_src[2] + e_in[2]
    e_copy(3).start()
    e_copy(4).start()
    e_copy(5).start()
    red.third(1)
    red.fifth(5)
    red.third(8)
    red.fourth(7)
    red.fifth(6)
    red.fifth(1)
    red.sixth(4)
    red.fifth(7)
    red.fourth(3)
    red.sixth(0)
    red.fifth(3)
    red.fourth(8)
    red.sixth(6)
    red.fifth(8)
    red.sixth(7)
    red.sixth(1)
    red.sixth(5)
    red.sixth(3)
    red.sixth(8)
    for n in range(3, 6):
        e_copy(n).wait_recv()
    e_src[4] = e_src[3] + e_in[3] + e_in[4] + e_in[5]
    ev_out = pltpu.make_async_copy(e_src.at[4], evec_out, osem.at[2])
    ev_out.start()
    ig_over.wait_recv()
    ig_own.wait()
    gmid[0] = ig_in[...].astype(F32)
    ig_there = pltpu.make_async_copy(gmid.at[0], igrad_ref.at[1 - p.x], osem.at[1])
    ig_there.start()
    out_own.wait()
    out_there.wait_recv()
    for c in range(g.shape[0]):
        red.last(c)
    for i in range(blocks):
        y_copy(i).wait_send()
        t_copy(i).wait_send()
    for n in range(2):
        o_copy(n).wait_send()
        u_copy(n).wait_send()
    out_over.wait_send()
    ig_over.wait_send()
    for n in range(6):
        e_copy(n).wait_send()
    for gather in gathers:
        gather.drain()
    swap.drain()
    cot_swap.drain()
    for d in (1, 3, 2):
        extra_copy(d, False).wait_send()
    ev_out.wait()
    ig_there.wait()


def layer(inputs, positions, wq, wk, wv, wo_t, win, wout_t, extra_in, cotangent):
    D, INNER, FF = win.shape[0] * lax.axis_size("fsdp"), wo_t.shape[1], win.shape[1]
    half, ffh, shard = INNER // 2, FF // 2, wq.shape[0]
    B = inputs.shape[1]
    R = inputs.shape[0] * B * 2
    heads, pairs = half // 64, half // T
    width = 4 * half + 2 * ffh
    piece, FW = shard // 4, 512
    nc = width // FW
    zf = 2
    sds = jax.ShapeDtypeStruct
    any_ = pl.BlockSpec(memory_space=pl.ANY)
    vm = pl.BlockSpec(memory_space=pltpu.VMEM)
    sem = pltpu.SemaphoreType.DMA
    V = pltpu.VMEM
    return pl.pallas_call(
        layer_kernel,
        in_specs=[any_, vm] + [any_] * 8,
        out_specs=[any_] * 5,
        out_shape=[
            sds(inputs.shape, BF), sds(inputs.shape, F32), sds((2, nc, 4, piece, FW), BF), sds((24, T), F32), sds((pairs, 2, R, R), BF),
        ],
        scratch_shapes=[
            V((D, width), BF), V((R, D), BF), V((R, D), BF), V((D, T), BF), V((D, R), BF), V((D, R), BF),
            V((pairs, R, T), BF), V((pairs, R, T), BF), V((pairs, R, T), BF), V((pairs, R, T), BF), V((pairs, R, T), F32), V((T, T), F32),
            V((R, heads * 3 * T), BF), V((R, 3 * T), jnp.int32),
            V((2, R, T), BF), V((2, R, T), BF), V((2, 2, 256, R), BF),
            V((R, D), BF), V((R, D), BF), V((2, B, D), BF), V((4, B, D), BF),
            V((R, ffh), BF), V((2, B, D), F32), V((T, R), F32), V((T, R), F32),
            V((R, 3 * half), BF), V((R, D), BF), V((B, D), BF),
            V((heads, 8, T), F32), V((heads, 8, T), F32), V((8, D), F32), V((5, 24, T), F32), V((6, 24, T), F32),
            V((nc, 2, 2, 4, piece, FW), BF), V((nc - zf, 2, 2, 4, piece, FW // 2), BF), V((nc - zf, 2, 4, piece, FW // 2), BF),
            V((nc - zf, 3, piece, FW), BF), V((zf, 2, 2, 1, piece, FW // 2), BF), V((zf, 2, 1, piece, FW // 2), BF),
            V((zf, 3, 2, 2, piece, FW), BF), V((nc, piece, FW), BF),
            sem((10, 15)), sem((10, 15)), sem((3,)), sem((3,)), sem((3,)), sem((3,)), sem((3,)), sem((3,)), sem((12,)), sem((2,)),
            sem((4,)), sem((4,)), sem((4,)), sem((4,)), sem((2,)), sem((2,)), sem((2,)), sem((2,)), sem((2,)), sem((2,)), sem((6,)), sem((6,)),
            sem((nc, 10)), sem((nc, 10)), sem((nc,)), sem((3,)),
        ],
        compiler_params=pltpu.CompilerParams(collective_id=0, has_side_effects=True, vmem_limit_bytes=63 * 2**20),
        name="layer",
    )(inputs, positions, wq, wk, wv, wo_t, win, wout_t, extra_in, cotangent)


def fast_device(inputs, positions, w_query, w_key, w_value, w_output, gain_attn, rel_table, w_in, w_out, gain_ffn, cotangent):
    shard = gain_attn.shape[0]
    buckets, heads = rel_table.shape
    padded = jnp.pad(rel_table, ((0, shard - buckets), (0, T - 2 - heads)))
    extra = jnp.concatenate([gain_attn[:, None], gain_ffn[:, None], padded], axis=1)
    out, igrad, gfin, evec, _ = layer(inputs, positions, w_query, w_key, w_value, w_output.T, w_in, w_out.T, extra, cotangent)
    gf = gfin.reshape(2, gfin.shape[1], shard, -1).astype(jnp.float32)

    def wide(first, count):
        return jnp.concatenate([gf[core, c] for core in range(2) for c in range(first, first + count)], axis=1)

    def cols(m):
        return jnp.concatenate([gf[core, c][:, m * T : (m + 1) * T] for core in range(2) for c in range(6, 9)], axis=1)

    z = lax.axis_index("fsdp")
    tiles = evec.shape[1]
    gains = evec[:12].reshape(2, -1)
    g_gain = lax.dynamic_slice_in_dim(gains, z * shard, shard, 1)
    g_table = lax.dynamic_slice_in_dim(evec[12:24], z * buckets, buckets, 1).T
    return (
        out, igrad, cols(0), cols(1), cols(2), cols(3).T, g_gain[0], g_table, wide(3, 3), wide(0, 3).T, g_gain[1],
    )


def rms_norm(values, gain):
    return values * lax.rsqrt(jnp.mean(values * values, axis=-1, keepdims=True) + EPS) * gain


def bias_onehot(query_positions, key_places, bucket_count):
    buckets = bucket_of(key_places[:, None, :] - query_positions[:, :, None])
    labels = lax.broadcasted_iota(jnp.int32, (1, bucket_count, 1, 1), 1)
    return (buckets[:, None, :, :] == labels).astype(jnp.bfloat16)


def split_heads(rows, head_count):
    return rows.reshape(rows.shape[0], rows.shape[1], head_count, -1)


def block_scores(query_rows, key_rows, onehot, table_b):
    head_count = table_b.shape[1]
    scores = jnp.einsum(
        "sqhd,skhd->shqk",
        split_heads(query_rows, head_count),
        split_heads(key_rows, head_count),
        preferred_element_type=jnp.float32,
    )
    bias_term = jnp.einsum("sbqk,bh->shqk", onehot, table_b, preferred_element_type=jnp.float32)
    return scores + bias_term


def pair_grads(
    query_rows,
    grad_rows,
    logsum,
    row_products,
    query_positions,
    key_rows,
    value_rows,
    key_places,
    table_b,
):
    head_count = table_b.shape[1]
    onehot = bias_onehot(query_positions, key_places, table_b.shape[0])
    scores = block_scores(query_rows, key_rows, onehot, table_b)
    probs = jnp.exp(scores - logsum[..., None])
    grad_heads = split_heads(grad_rows, head_count)
    dprobs = jnp.einsum(
        "sqhd,skhd->shqk",
        grad_heads,
        split_heads(value_rows, head_count),
        preferred_element_type=jnp.float32,
    )
    grad_scores = (probs * (dprobs - row_products[..., None])).astype(jnp.bfloat16)
    grad_query = jnp.einsum(
        "shqk,skhd->sqhd",
        grad_scores,
        split_heads(key_rows, head_count),
        preferred_element_type=jnp.float32,
    )
    grad_key = jnp.einsum(
        "shqk,sqhd->skhd",
        grad_scores,
        split_heads(query_rows, head_count),
        preferred_element_type=jnp.float32,
    )
    grad_value = jnp.einsum(
        "shqk,sqhd->skhd",
        probs.astype(jnp.bfloat16),
        grad_heads,
        preferred_element_type=jnp.float32,
    )
    grad_table = jnp.einsum(
        "sbqk,shqk->bh", onehot, grad_scores, preferred_element_type=jnp.float32
    )
    return (
        grad_query.reshape(query_rows.shape),
        grad_key.reshape(key_rows.shape),
        grad_value.reshape(value_rows.shape),
        grad_table,
    )


def add_rows(whole, first_row, added_term):
    current = lax.dynamic_slice_in_dim(whole, first_row, added_term.shape[1], 1)
    return lax.dynamic_update_slice_in_dim(whole, current + added_term, first_row, 1)


def project_rows(left_operand, right_operand):
    return jnp.dot(left_operand, right_operand, preferred_element_type=jnp.float32)


def outer_sum(left_operand, right_operand):
    return jnp.einsum("nf,nd->fd", left_operand, right_operand, preferred_element_type=jnp.float32)


def general_device(
    inputs,
    positions,
    w_query,
    w_key,
    w_value,
    w_output,
    gain_attn,
    rel_table,
    w_in,
    w_out,
    gain_ffn,
    cotangent,
):
    groups, block_rows, model_width = inputs.shape
    head_count = rel_table.shape[1]
    tokens = groups * block_rows
    query_w, key_w, value_w, output_w, gain_one, table_b = (
        lax.all_gather(w_query, "fsdp", axis=0, tiled=True),
        lax.all_gather(w_key, "fsdp", axis=0, tiled=True),
        lax.all_gather(w_value, "fsdp", axis=0, tiled=True),
        lax.all_gather(w_output, "fsdp", axis=1, tiled=True),
        lax.all_gather(gain_attn, "fsdp", axis=0, tiled=True),
        lax.all_gather(rel_table, "fsdp", axis=0, tiled=True),
    )
    in_w, out_w, gain_two = (
        lax.all_gather(w_in, "fsdp", axis=0, tiled=True),
        lax.all_gather(w_out, "fsdp", axis=1, tiled=True),
        lax.all_gather(gain_ffn, "fsdp", axis=0, tiled=True),
    )
    gain_one_f = gain_one.astype(jnp.float32)
    gain_two_f = gain_two.astype(jnp.float32)
    own_first = lax.axis_index("ctx") * block_rows
    query_positions = lax.dynamic_slice_in_dim(positions, own_first, block_rows, 1)
    flat_inputs = inputs.reshape(tokens, model_width).astype(jnp.float32)
    normed = rms_norm(flat_inputs, gain_one_f).astype(jnp.bfloat16)
    queries = project_rows(normed, query_w).astype(jnp.bfloat16).reshape(groups, block_rows, -1)
    key_block = project_rows(normed, key_w).astype(jnp.bfloat16).reshape(groups, block_rows, -1)
    value_block = project_rows(normed, value_w).astype(jnp.bfloat16).reshape(groups, block_rows, -1)
    inner_width = queries.shape[2]
    head_size = inner_width // head_count
    start_state = (
        jnp.full((groups, head_count, block_rows), -1e30, jnp.float32),
        jnp.zeros((groups, head_count, block_rows), jnp.float32),
        jnp.zeros((groups, block_rows, head_count, head_size), jnp.float32),
    )
    key_piece = lax.all_gather(key_block, "ctx", axis=1, tiled=True)
    value_portion = lax.all_gather(value_block, "ctx", axis=1, tiled=True)
    piece_rows = key_piece.shape[1]
    step_rows = math.gcd(piece_rows, block_rows)

    def forward_inner_step(block_index, state):
        running, total, weighted = state
        offset = block_index * step_rows
        key_part = lax.dynamic_slice_in_dim(key_piece, offset, step_rows, 1)
        value_part = lax.dynamic_slice_in_dim(value_portion, offset, step_rows, 1)
        key_places = lax.dynamic_slice_in_dim(positions, offset, step_rows, 1)
        onehot = bias_onehot(query_positions, key_places, table_b.shape[0])
        scores = block_scores(queries, key_part, onehot, table_b)
        newest = jnp.maximum(running, jnp.max(scores, axis=-1))
        factor = jnp.exp(running - newest)
        weights = jnp.exp(scores - newest[..., None])
        total = total * factor + jnp.sum(weights, axis=-1)
        update = jnp.einsum(
            "shqk,skhd->sqhd",
            weights.astype(jnp.bfloat16),
            split_heads(value_part, head_count),
            preferred_element_type=jnp.float32,
        )
        weighted = weighted * jnp.transpose(factor, (0, 2, 1))[..., None] + update
        return (newest, total, weighted)

    running, total, weighted = lax.fori_loop(
        0, piece_rows // step_rows, forward_inner_step, start_state
    )
    logsum = running + jnp.log(total)
    mixed = weighted / jnp.transpose(total, (0, 2, 1))[..., None]
    mixed_b = mixed.reshape(tokens, inner_width).astype(jnp.bfloat16)
    middle = flat_inputs + project_rows(mixed_b, output_w)
    normed_two = rms_norm(middle, gain_two_f).astype(jnp.bfloat16)
    hidden = project_rows(normed_two, in_w)
    active = jax.nn.gelu(hidden).astype(jnp.bfloat16)
    result = middle + project_rows(active, out_w)
    output = result.astype(jnp.bfloat16).reshape(inputs.shape)
    grad_top = cotangent.reshape(tokens, model_width).astype(jnp.float32)
    grad_branch = grad_top.astype(jnp.bfloat16)
    grad_out_w = outer_sum(active, grad_branch)
    grad_active = lax.dot_general(
        grad_branch, out_w, (((1,), (1,)), ((), ())), preferred_element_type=jnp.float32
    )
    gelu_pull = jax.vjp(jax.nn.gelu, hidden)[1]
    grad_hidden = gelu_pull(grad_active)[0].astype(jnp.bfloat16)
    grad_in_w = outer_sum(normed_two, grad_hidden)
    grad_normed_two = lax.dot_general(
        grad_hidden, in_w, (((1,), (1,)), ((), ())), preferred_element_type=jnp.float32
    )
    norm_pull = jax.vjp(rms_norm, middle, gain_two_f)[1]
    grad_from_norm, grad_gain_two = norm_pull(grad_normed_two)
    grad_middle = grad_top + grad_from_norm
    ffn_parts = (
        lax.psum_scatter(
            grad_in_w.astype(jnp.bfloat16), "fsdp", scatter_dimension=0, tiled=True
        ).astype(jnp.float32),
        lax.psum_scatter(
            grad_out_w.astype(jnp.bfloat16), "fsdp", scatter_dimension=1, tiled=True
        ).astype(jnp.float32),
        lax.psum_scatter(
            grad_gain_two.astype(jnp.bfloat16), "fsdp", scatter_dimension=0, tiled=True
        ).astype(jnp.float32),
    )
    ffn_parts = (
        lax.psum(ffn_parts[0].astype(jnp.bfloat16), ("seq", "ctx")).astype(jnp.float32),
        lax.psum(ffn_parts[1].astype(jnp.bfloat16), ("seq", "ctx")).astype(jnp.float32),
        lax.psum(ffn_parts[2].astype(jnp.bfloat16), ("seq", "ctx")).astype(jnp.float32),
    )
    grad_y = grad_middle.astype(jnp.bfloat16)
    grad_output_w = outer_sum(mixed_b, grad_y)
    grad_mixed = (
        lax.dot_general(
            grad_y, output_w, (((1,), (1,)), ((), ())), preferred_element_type=jnp.float32
        )
        .astype(jnp.bfloat16)
        .reshape(groups, block_rows, inner_width)
    )
    row_products = jnp.transpose(
        jnp.sum(split_heads(grad_mixed.astype(jnp.float32), head_count) * mixed, axis=-1), (0, 2, 1)
    )
    table_zero = jnp.zeros(table_b.shape, jnp.float32)
    seq_rows = block_rows * lax.axis_size("ctx")
    whole_zero = jnp.zeros((groups, seq_rows, inner_width), jnp.float32)
    start_back = (
        jnp.zeros((groups, block_rows, inner_width), jnp.float32),
        whole_zero,
        whole_zero,
        table_zero,
    )
    keys_key_piece = lax.all_gather(key_block, "ctx", axis=1, tiled=True)
    keys_value_portion = lax.all_gather(value_block, "ctx", axis=1, tiled=True)
    piece_rows = keys_key_piece.shape[1]
    keys_step_rows = math.gcd(piece_rows, block_rows)

    def keys_inner_step(block_index, state):
        query_total, key_total, value_total, table_total = state
        offset = block_index * keys_step_rows
        key_part = lax.dynamic_slice_in_dim(keys_key_piece, offset, keys_step_rows, 1)
        value_part = lax.dynamic_slice_in_dim(keys_value_portion, offset, keys_step_rows, 1)
        key_places = lax.dynamic_slice_in_dim(positions, offset, keys_step_rows, 1)
        grad_q, grad_k, grad_v, grad_t = pair_grads(
            queries,
            grad_mixed,
            logsum,
            row_products,
            query_positions,
            key_part,
            value_part,
            key_places,
            table_b,
        )
        return (
            query_total + grad_q,
            add_rows(key_total, offset, grad_k),
            add_rows(value_total, offset, grad_v),
            table_total + grad_t,
        )

    grad_query, key_whole, value_whole, grad_table = lax.fori_loop(
        0, piece_rows // keys_step_rows, keys_inner_step, start_back
    )
    grad_key, grad_value = (
        lax.psum_scatter(
            key_whole.astype(jnp.bfloat16), "ctx", scatter_dimension=1, tiled=True
        ).astype(jnp.float32),
        lax.psum_scatter(
            value_whole.astype(jnp.bfloat16), "ctx", scatter_dimension=1, tiled=True
        ).astype(jnp.float32),
    )
    query_b = grad_query.reshape(tokens, inner_width).astype(jnp.bfloat16)
    key_b = grad_key.reshape(tokens, inner_width).astype(jnp.bfloat16)
    value_b = grad_value.reshape(tokens, inner_width).astype(jnp.bfloat16)
    grad_query_w = outer_sum(normed, query_b)
    grad_key_w = outer_sum(normed, key_b)
    grad_value_w = outer_sum(normed, value_b)
    contract = (((1,), (1,)), ((), ()))
    grad_normed = lax.dot_general(query_b, query_w, contract, preferred_element_type=jnp.float32)
    grad_normed = grad_normed + lax.dot_general(
        key_b, key_w, contract, preferred_element_type=jnp.float32
    )
    grad_normed = grad_normed + lax.dot_general(
        value_b, value_w, contract, preferred_element_type=jnp.float32
    )
    first_pull = jax.vjp(rms_norm, flat_inputs, gain_one_f)[1]
    grad_from_first, grad_gain_one = first_pull(grad_normed)
    input_grad = (grad_middle + grad_from_first).reshape(inputs.shape)
    attn_parts = (
        lax.psum_scatter(
            grad_query_w.astype(jnp.bfloat16), "fsdp", scatter_dimension=0, tiled=True
        ).astype(jnp.float32),
        lax.psum_scatter(
            grad_key_w.astype(jnp.bfloat16), "fsdp", scatter_dimension=0, tiled=True
        ).astype(jnp.float32),
        lax.psum_scatter(
            grad_value_w.astype(jnp.bfloat16), "fsdp", scatter_dimension=0, tiled=True
        ).astype(jnp.float32),
        lax.psum_scatter(
            grad_output_w.astype(jnp.bfloat16), "fsdp", scatter_dimension=1, tiled=True
        ).astype(jnp.float32),
        lax.psum_scatter(
            grad_gain_one.astype(jnp.bfloat16), "fsdp", scatter_dimension=0, tiled=True
        ).astype(jnp.float32),
        lax.psum_scatter(
            grad_table.astype(jnp.bfloat16), "fsdp", scatter_dimension=0, tiled=True
        ).astype(jnp.float32),
    )
    attn_parts = (
        lax.psum(attn_parts[0].astype(jnp.bfloat16), ("seq", "ctx")).astype(jnp.float32),
        lax.psum(attn_parts[1].astype(jnp.bfloat16), ("seq", "ctx")).astype(jnp.float32),
        lax.psum(attn_parts[2].astype(jnp.bfloat16), ("seq", "ctx")).astype(jnp.float32),
        lax.psum(attn_parts[3].astype(jnp.bfloat16), ("seq", "ctx")).astype(jnp.float32),
        lax.psum(attn_parts[4].astype(jnp.bfloat16), ("seq", "ctx")).astype(jnp.float32),
        lax.psum(attn_parts[5].astype(jnp.bfloat16), ("seq", "ctx")).astype(jnp.float32),
    )
    return (
        output,
        input_grad,
        attn_parts[0],
        attn_parts[1],
        attn_parts[2],
        attn_parts[3],
        attn_parts[4],
        attn_parts[5],
        ffn_parts[0],
        ffn_parts[1],
        ffn_parts[2],
    )


def solution(mesh):
    in_specs = (
        P(("seq", "fsdp"), "ctx", None),
        P(("seq", "fsdp"), None),
        P("fsdp", None),
        P("fsdp", None),
        P("fsdp", None),
        P(None, "fsdp"),
        P("fsdp"),
        P("fsdp", None),
        P("fsdp", None),
        P(None, "fsdp"),
        P("fsdp"),
        P(("seq", "fsdp"), "ctx", None),
    )
    out_specs = (
        P(("seq", "fsdp"), "ctx", None),
        P(("seq", "fsdp"), "ctx", None),
        P("fsdp", None),
        P("fsdp", None),
        P("fsdp", None),
        P(None, "fsdp"),
        P("fsdp"),
        P("fsdp", None),
        P("fsdp", None),
        P(None, "fsdp"),
        P("fsdp"),
    )
    fits = mesh.shape["seq"] == 2 and mesh.shape["ctx"] == 4 and mesh.shape["fsdp"] == 4
    per_device = fast_device if fits else general_device
    return jax.shard_map(
        per_device, mesh=mesh, in_specs=in_specs, out_specs=out_specs, check_vma=False
    )
```

profile of v0, /device:TPU:0, one launch (start us, length us, event | category | flops | bytes accessed | tf_op | source)
XLA Modules:
  0.0 189.9 jit_solution(9236708343058541852)
XLA Ops:
  0.6 0.7 broadcast_in_dim.8
  1.4 0.7 broadcast_in_dim.9
  2.1 1.4 fusion.13.extra_in
  3.5 175.1 %layer.1 = (bf16[2,256,768]{2,1,0:T(8,128)(2,1)}, f32[2,256,768]{2,1,0:T(8,128)}, bf16[2,9,4,48,512]{4,3,2,1,0:T(8,128)(2,1)}, f32[24,128]{1,0:T(8,128)}, bf16[3,2,1024,1024]{3,2,1,0:T(8,128)(2,1)}) custom-call(bf16[2,256,768]{2,1,0:T(8,128)(2,1)} %inputs.1, s32[2,1024]{1,0:T(2,128)} %positions.1, bf16[192,768]{1,0:T(8,128)(2,1)} %wq.1, ...), custom_call_target="tpu_custom_call" | custom-call | tf_op jit(solution)/shard_map/layer/pallas_call | solution.py:1016
  178.6 3.0 %bitcast_convert_fusion = f32[2,9,192,512]{3,2,1,0:T(8,128)S(1)} fusion(bf16[2,9,4,48,512]{4,3,2,1,0:T(8,128)(2,1)} %get-tuple-element.17), kind=kLoop, calls=%fused_computation | loop fusion | flops 1769472 | bytes 10616832 | tf_op jit(solution)/shard_map/convert_element_type | solution.py:1050
  181.6 0.1 fusion.5
  181.7 0.1 fusion.4
  181.7 0.1 fusion.3
  181.8 0.1 fusion.2
  181.9 0.1 fusion.1
  181.9 0.1 fusion
  182.0 0.0 copy-start.2
  182.0 0.0 copy-start.3
  182.0 1.4 copy-done.2
  183.4 0.8 copy-done.3
  184.2 0.2 slice_bitcast_fusion.12
  184.4 0.0 copy-start.4
  184.4 0.0 copy-start.1
  184.5 0.0 copy-start
  184.6 0.0 copy-start.6
  184.6 0.8 copy-done.6
  185.4 0.0 copy-start.7
  185.4 0.0 copy-start.8
  185.4 0.0 copy-start.5
  185.4 0.8 copy-done.7
  186.3 0.2 copy-done.8
  186.5 0.0 copy-done.4
  186.5 0.6 fusion.15
  187.1 0.1 dynamic-slice_bitcast_fusion
  187.2 0.7 copy.26
  187.9 0.0 copy-done.1
  187.9 0.9 copy.59
  188.7 0.0 copy-done
  188.7 1.1 copy.60
  189.9 0.0 copy-done.5
  (8 shorter events, 0.2 us)
Async XLA Ops:
  182.0 1.4 copy-start.2
  182.0 2.2 %copy-start.3 = (f32[192,3072]{1,0:T(8,128)}, f32[192,3072]{1,0:T(8,128)S(1)}, u32[]{:S(2)}) copy-start(f32[192,3072]{1,0:T(8,128)S(1)} %get-tuple-element.106) | copy-start | bytes 7077892
  184.4 2.1 %copy-start.4 = (f32[24,128]{1,0:T(8,128)S(1)}, f32[24,128]{1,0:T(8,128)}, u32[]{:S(2)}) copy-start(f32[24,128]{1,0:T(8,128)} %get-tuple-element.18) | copy-start | bytes 36868
  184.4 3.5 %copy-start.1 = (bf16[2,256,768]{2,1,0:T(8,128)(2,1)S(1)}, bf16[2,256,768]{2,1,0:T(8,128)(2,1)}, u32[]{:S(2)}) copy-start(bf16[2,256,768]{2,1,0:T(8,128)(2,1)} %get-tuple-element.98) | copy-start | bytes 2359300
  184.5 4.3 %copy-start = (f32[2,256,768]{2,1,0:T(8,128)S(1)}, f32[2,256,768]{2,1,0:T(8,128)}, u32[]{:S(2)}) copy-start(f32[2,256,768]{2,1,0:T(8,128)} %get-tuple-element.99) | copy-start | bytes 4718596
  184.6 0.8 copy-start.6
  185.4 0.8 copy-start.7
  185.4 1.0 copy-start.8
  185.4 4.4 %copy-start.5 = (f32[192,768]{1,0:T(8,128)}, f32[192,768]{1,0:T(8,128)S(1)}, u32[]{:S(2)}) copy-start(f32[192,768]{1,0:T(8,128)S(1)} %get-tuple-element.59) | copy-start | bytes 1769476
where the time goes:
time: 190 us
  Pallas kernels  175 us (92%)
  local copies, waits for them, and re-layouts  9.62 us (5%)
  other arithmetic  4.39 us (2%)
    pallas_call x1, Pallas kernels, layer(): pl.pallas_call(layer_kernel, in_specs=[any_, vm] + [any_] * 8, out_specs=...  175 us
    unnamed x31, local copies, waits for them, and re-layouts  7.11 us

commit v1 on v0

--- a/solution.py
+++ b/solution.py
@@ -452,14 +452,12 @@
     band = [(a, d) for a in range(nt) for d in range(3) if 0 <= a + d - 1 < nt]
     cols = {}
     early = {
-        25: [gathers[1].pass_z],
-        9: [gathers[0].pass_z],
-        37: [gathers[0].pass_plane],
+        36: [gathers[0].pass_plane, gathers[1].pass_plane],
+        40: [swap.relay],
+        34: [gathers[1].pass_z, gathers[2].pass_z],
         43: [gathers[2].pass_plane],
-        42: [swap.relay],
+        23: [gathers[0].pass_z],
         44: [gathers[3].pass_z, gathers[4].pass_z],
-        41: [gathers[1].pass_plane],
-        27: [gathers[2].pass_z],
     }
 
     def offsets(a, d):
@@ -538,10 +536,10 @@
         1: [gathers[5].pass_z],
         3: [gathers[6].pass_z],
         5: [gathers[4].pass_plane],
-        13: [gathers[8].pass_z],
+        13: [cot_swap.relay, gathers[8].pass_z],
         4: [gathers[3].pass_plane, gathers[5].pass_plane],
         6: [gathers[6].pass_plane, cot_swap.start],
-        9: [gathers[7].pass_z],
+        8: [gathers[7].pass_z],
     }
     for step in ahead.get(-1, ()):
         step()
@@ -646,7 +644,6 @@
     between = {
         1: [gathers[7].pass_plane],
         3: [gathers[8].pass_plane],
-        0: [cot_swap.relay],
     }
 
     def during(i, base, table):
@@ -696,8 +693,7 @@
         gather.finish()
     later = {
         2: [functools.partial(red.second, 2)],
-        4: [functools.partial(red.third, 2)],
-        10: [functools.partial(red.gathered_z, 0)],
+        9: [functools.partial(red.second, 3)],
     }
 
     def ffn_back(i, carry):
@@ -777,9 +773,12 @@
 
     p_load(0, 0).start()
     stages = {
-        1: [functools.partial(red.second, 4)],
-        9: [functools.partial(red.second, 5), functools.partial(red.gathered_z, 1)],
-        11: [functools.partial(red.fourth, 2), functools.partial(red.second, 3), functools.partial(red.second, 7), functools.partial(red.second, 0), functools.partial(red.third, 4), functools.partial(red.second, 6)],
+        4: [functools.partial(red.second, 4)],
+        5: [functools.partial(red.gathered_z, 0)],
+        6: [functools.partial(red.third, 2)],
+        7: [functools.partial(red.third, 3)],
+        8: [functools.partial(red.second, 6), functools.partial(red.fourth, 2), functools.partial(red.third, 4), functools.partial(red.second, 5)],
+        11: [functools.partial(red.fourth, 3), functools.partial(red.second, 7), functools.partial(red.second, 0)],
     }
 
     def lanes_of(m, hp):
@@ -874,11 +873,10 @@
         rows = pl.ds(pl.multiple_of((2 * n + 1 - p.core) * B, B), B)
         slope[(2 + n) * B : (3 + n) * B, :D] = dot_nt(cat[rows, :], w[:, :c_o]).astype(BF)
         u_copy(n).start()
-    red.third(0)
-    red.second(1)
     red.fifth(2)
-    red.third(7)
-    red.third(5)
+    red.fifth(3)
+    red.fourth(4)
+    red.third(6)
     for n in range(2):
         rows = pl.ds(pl.multiple_of((2 * n + p.core) * B, B), B)
         t = dot_nt(cat[rows, :], w[:, :c_o])
@@ -923,46 +921,46 @@
         device = (p.sib, p.xn, p.yn, p.zn(1), p.zn(2), p.zn(3))[n]
         return remote(e_src.at[min(n, 3)], e_in.at[n], ev_s.at[n], ev_r.at[n], device)
 
-    red.third(6)
     ig_over.start()
     e_copy(0).start()
     e_copy(0).wait_recv()
     e_src[1] = e_src[0] + e_in[0]
     e_copy(1).start()
-    red.fourth(4)
-    red.fourth(5)
+    red.third(5)
+    red.third(0)
+    red.fifth(4)
+    red.gathered_z(1)
     red.sixth(2)
-    red.fifth(0)
-    red.third(3)
     red.second(8)
+    red.fourth(6)
+    red.third(7)
     e_copy(1).wait_recv()
     e_src[2] = e_src[1] + e_in[1]
     e_copy(2).start()
-    red.fifth(4)
-    red.fourth(6)
+    red.sixth(3)
+    red.fourth(7)
     e_copy(2).wait_recv()
     e_src[3] = e_src[2] + e_in[2]
     e_copy(3).start()
     e_copy(4).start()
     e_copy(5).start()
+    red.fifth(0)
+    red.fourth(5)
+    red.second(1)
+    red.third(8)
+    red.fifth(6)
+    red.fifth(7)
+    red.fifth(5)
     red.third(1)
-    red.fifth(5)
-    red.third(8)
-    red.fourth(7)
-    red.fifth(6)
+    red.sixth(6)
+    red.fourth(8)
     red.fifth(1)
+    red.sixth(7)
+    red.fifth(8)
+    red.sixth(5)
+    red.sixth(0)
+    red.sixth(1)
     red.sixth(4)
-    red.fifth(7)
-    red.fourth(3)
-    red.sixth(0)
-    red.fifth(3)
-    red.fourth(8)
-    red.sixth(6)
-    red.fifth(8)
-    red.sixth(7)
-    red.sixth(1)
-    red.sixth(5)
-    red.sixth(3)
     red.sixth(8)
     for n in range(3, 6):
         e_copy(n).wait_recv()
@@ -1041,28 +1039,90 @@
     )(inputs, positions, wq, wk, wv, wo_t, win, wout_t, extra_in, cotangent)
 
 
+def finish_kernel(gfin, out_in, ig_in, wq, wk, wv, wo_t, win, wout_t, out, ig, gv, fa, fw, ob, ib, lsem, osem):
+    cores, chunks, cols, piece, width = gv.shape
+    half, third = fa.shape[2] // 2, fw.shape[2] // 2
+    order = [(part, core) for part in range(3) for core in range(cores)]
+    loads = [
+        pltpu.make_async_copy(gfin.at[core, pl.ds(part * 3, 3)], gv.at[core, pl.ds(part * 3, 3)], lsem.at[n])
+        for n, (part, core) in enumerate(order)
+    ]
+    through = [
+        (pltpu.make_async_copy(a, b, lsem.at[len(order) + n]), pltpu.make_async_copy(b, c, osem.at[n]))
+        for n, (a, b, c) in enumerate(((ig_in, ib, ig), (out_in, ob, out)))
+    ]
+    loads[0].start()
+    for load, _ in through:
+        load.start()
+    for load in loads[1:]:
+        load.start()
+    stores = []
+    for n, (part, core) in enumerate(order):
+        loads[n].wait()
+
+        def widen(col, carry):
+            rows = pl.ds(pl.multiple_of(col * piece, 16), piece)
+            for c in range(3):
+                value = gv[core, part * 3 + c, col].astype(F32)
+                if part < 2:
+                    first = core * third + c * width
+                    fw[part, rows, first : first + width] = value
+                else:
+                    first = core * half + c * T
+                    for m in range(4):
+                        fa[m, rows, first : first + T] = value[:, m * T : (m + 1) * T]
+            return carry
+
+        lax.fori_loop(0, cols, widen, 0)
+        if part < 2:
+            lanes = pl.ds(core * third, third)
+            stores.append(pltpu.make_async_copy(fw.at[part, :, lanes], (wout_t, win)[part].at[:, lanes], osem.at[2 + n]))
+            stores[-1].start()
+        if n == 0:
+            for load, store in through:
+                load.wait()
+                store.start()
+                stores.append(store)
+    for m, ref in enumerate((wq, wk, wv, wo_t)):
+        stores.append(pltpu.make_async_copy(fa.at[m], ref, osem.at[6 + m]))
+        stores[-1].start()
+    for store in stores:
+        store.wait()
+
+
+def finish(gfin, out, igrad):
+    cores, chunks, cols, piece, width = gfin.shape
+    shard, d, ff = cols * piece, cols * piece * 4, cores * 3 * width
+    sds = jax.ShapeDtypeStruct
+    any_ = pl.BlockSpec(memory_space=pl.ANY)
+    return pl.pallas_call(
+        finish_kernel,
+        in_specs=[any_] * 3,
+        out_specs=[any_] * 8,
+        out_shape=[sds((shard, d), F32)] * 4 + [sds((shard, ff), F32)] * 2 + [sds(out.shape, BF), sds(igrad.shape, F32)],
+        scratch_shapes=[
+            pltpu.VMEM(gfin.shape, BF), pltpu.VMEM((4, shard, d), F32), pltpu.VMEM((2, shard, ff), F32),
+            pltpu.VMEM(out.shape, BF), pltpu.VMEM(igrad.shape, F32),
+            pltpu.SemaphoreType.DMA((8,)), pltpu.SemaphoreType.DMA((10,)),
+        ],
+        compiler_params=pltpu.CompilerParams(vmem_limit_bytes=60 * 2**20),
+        name="finish",
+    )(gfin, out, igrad)
+
+
 def fast_device(inputs, positions, w_query, w_key, w_value, w_output, gain_attn, rel_table, w_in, w_out, gain_ffn, cotangent):
     shard = gain_attn.shape[0]
     buckets, heads = rel_table.shape
     padded = jnp.pad(rel_table, ((0, shard - buckets), (0, T - 2 - heads)))
     extra = jnp.concatenate([gain_attn[:, None], gain_ffn[:, None], padded], axis=1)
     out, igrad, gfin, evec, _ = layer(inputs, positions, w_query, w_key, w_value, w_output.T, w_in, w_out.T, extra, cotangent)
-    gf = gfin.reshape(2, gfin.shape[1], shard, -1).astype(jnp.float32)
-
-    def wide(first, count):
-        return jnp.concatenate([gf[core, c] for core in range(2) for c in range(first, first + count)], axis=1)
-
-    def cols(m):
-        return jnp.concatenate([gf[core, c][:, m * T : (m + 1) * T] for core in range(2) for c in range(6, 9)], axis=1)
-
+    g_q, g_k, g_v, g_o, g_in, g_out, out, igrad = finish(gfin, out, igrad)
     z = lax.axis_index("fsdp")
     tiles = evec.shape[1]
     gains = evec[:12].reshape(2, -1)
     g_gain = lax.dynamic_slice_in_dim(gains, z * shard, shard, 1)
     g_table = lax.dynamic_slice_in_dim(evec[12:24], z * buckets, buckets, 1).T
-    return (
-        out, igrad, cols(0), cols(1), cols(2), cols(3).T, g_gain[0], g_table, wide(3, 3), wide(0, 3).T, g_gain[1],
-    )
+    return out, igrad, g_q, g_k, g_v, g_o.T, g_gain[0], g_table, g_in, g_out.T, g_gain[1]
 
 
 def rms_norm(values, gain):

time: 190 us -> 184 us (0.968)
  local copies, waits for them, and re-layouts: 9.62 us -> 2.9 us
  Pallas kernels: 175 us -> 179 us
  other arithmetic: 4.39 us -> 1.39 us
    unnamed x31 -> x3, local copies, waits for them, and re-layouts: 7.11 us -> 0.68 us
    pallas_call x0 -> x1, Pallas kernels: none -> 5.8 us  [finish(): pl.pallas_call(finish_kernel, in_specs=[any_] * 3, out_specs=[any_] * 8,...]
    convert_element_type x1 -> x0, other arithmetic: 2.99 us -> none  [fast_device(): gf = gfin.reshape(2, gfin.shape[1], shard, -1).astype(jnp.float32)]
where the time goes in v1:
time: 184 us
  Pallas kernels  179 us (97%)
  local copies, waits for them, and re-layouts  2.9 us (2%)
    pallas_call x1, Pallas kernels, layer(): pl.pallas_call(layer_kernel, in_specs=[any_, vm] + [any_] * 8, out_specs=...  173 us
    pallas_call x1, Pallas kernels, finish(): pl.pallas_call(finish_kernel, in_specs=[any_] * 3, out_specs=[any_] * 8,...  5.8 us

profile of v1, /device:TPU:0, one launch (start us, length us, event | category | flops | bytes accessed | tf_op | source)
XLA Modules:
  0.0 184.2 jit_solution(17402116200338394087)
XLA Ops:
  0.6 0.7 broadcast_in_dim.8
  1.4 0.7 broadcast_in_dim.9
  2.1 1.4 fusion.1.extra_in
  3.5 173.4 %layer.1 = (bf16[2,256,768]{2,1,0:T(8,128)(2,1)}, f32[2,256,768]{2,1,0:T(8,128)}, bf16[2,9,4,48,512]{4,3,2,1,0:T(8,128)(2,1)}, f32[24,128]{1,0:T(8,128)}, bf16[3,2,1024,1024]{3,2,1,0:T(8,128)(2,1)}) custom-call(bf16[2,256,768]{2,1,0:T(8,128)(2,1)} %inputs.1, s32[2,1024]{1,0:T(2,128)} %positions.1, bf16[192,768]{1,0:T(8,128)(2,1)} %wq.1, ...), custom_call_target="tpu_custom_call" | custom-call | tf_op jit(solution)/shard_map/layer/pallas_call | solution.py:1014
  176.9 0.0 copy-start
  176.9 5.8 %finish.1 = (f32[192,768]{1,0:T(8,128)}, f32[192,768]{1,0:T(8,128)}, f32[192,768]{1,0:T(8,128)}, f32[192,768]{1,0:T(8,128)}, f32[192,3072]{1,0:T(8,128)}, /*inde...) custom-call(bf16[2,9,4,48,512]{4,3,2,1,0:T(8,128)(2,1)} %get-tuple-element.23.gfin, ...), custom_call_target="tpu_custom_call" | custom-call | tf_op jit(solution)/shard_map/finish/pallas_call | solution.py:1098
  182.7 0.0 copy-done
  182.8 0.6 fusion.3
  183.4 0.1 dynamic-slice_bitcast_fusion
  183.5 0.7 copy.26
  (2 shorter events, 0.0 us)
Async XLA Ops:
  176.9 5.8 %copy-start = (f32[24,128]{1,0:T(8,128)S(1)}, f32[24,128]{1,0:T(8,128)}, u32[]{:S(2)}) copy-start(f32[24,128]{1,0:T(8,128)} %get-tuple-element.32) | copy-start | bytes 36868

commit v2 on v1

--- a/solution.py
+++ b/solution.py
@@ -857,8 +857,9 @@
         cat[:, lanes_of(1, hp)] = dk_acc[...].T.astype(BF)
         cat[:, lanes_of(2, hp)] = dv_acc[...].T.astype(BF)
         c = 6 + hp
-        for m in range(3):
-            keep_pieces(c, m * T, n_t[...], cat[:, lanes_of(m, hp)])
+        pair_qk = jnp.concatenate([cat[:, lanes_of(0, hp)], cat[:, lanes_of(1, hp)]], axis=1)
+        keep_pieces(c, 0, n_t[...], pair_qk)
+        keep_pieces(c, 2 * T, n_t[...], cat[:, lanes_of(2, hp)])
         keep_pieces(c, 3 * T, turned[...], mixed[hp])
         for trip in range(heads // 2):
             pl.when(hp == trip)(functools.partial(red.start, 6 + trip))

time: 184 us -> 184 us (level)
  no operation moved by 1% of the time
where the time goes in v2:
time: 184 us
  Pallas kernels  179 us (97%)
  local copies, waits for them, and re-layouts  2.9 us (2%)
    pallas_call x1, Pallas kernels, layer(): pl.pallas_call(layer_kernel, in_specs=[any_, vm] + [any_] * 8, out_specs=...  173 us
    pallas_call x1, Pallas kernels, finish(): pl.pallas_call(finish_kernel, in_specs=[any_] * 3, out_specs=[any_] * 8,...  5.8 us

profile of v2, /device:TPU:0, one launch (start us, length us, event | category | flops | bytes accessed | tf_op | source)
XLA Modules:
  0.0 184.2 jit_solution(2561312482263608744)
XLA Ops:
  0.6 0.7 broadcast_in_dim.8
  1.4 0.7 broadcast_in_dim.9
  2.1 1.4 fusion.1.extra_in
  3.5 173.4 %layer.1 = (bf16[2,256,768]{2,1,0:T(8,128)(2,1)}, f32[2,256,768]{2,1,0:T(8,128)}, bf16[2,9,4,48,512]{4,3,2,1,0:T(8,128)(2,1)}, f32[24,128]{1,0:T(8,128)}, bf16[3,2,1024,1024]{3,2,1,0:T(8,128)(2,1)}) custom-call(bf16[2,256,768]{2,1,0:T(8,128)(2,1)} %inputs.1, s32[2,1024]{1,0:T(2,128)} %positions.1, bf16[192,768]{1,0:T(8,128)(2,1)} %wq.1, ...), custom_call_target="tpu_custom_call" | custom-call | tf_op jit(solution)/shard_map/layer/pallas_call | solution.py:1015
  176.9 0.0 copy-start
  176.9 5.8 %finish.1 = (f32[192,768]{1,0:T(8,128)}, f32[192,768]{1,0:T(8,128)}, f32[192,768]{1,0:T(8,128)}, f32[192,768]{1,0:T(8,128)}, f32[192,3072]{1,0:T(8,128)}, /*inde...) custom-call(bf16[2,9,4,48,512]{4,3,2,1,0:T(8,128)(2,1)} %get-tuple-element.23.gfin, ...), custom_call_target="tpu_custom_call" | custom-call | tf_op jit(solution)/shard_map/finish/pallas_call | solution.py:1099
  182.7 0.0 copy-done
  182.8 0.6 fusion.3
  183.4 0.1 dynamic-slice_bitcast_fusion
  183.5 0.7 copy.26
  (2 shorter events, 0.0 us)
Async XLA Ops:
  176.9 5.8 %copy-start = (f32[24,128]{1,0:T(8,128)S(1)}, f32[24,128]{1,0:T(8,128)}, u32[]{:S(2)}) copy-start(f32[24,128]{1,0:T(8,128)} %get-tuple-element.32) | copy-start | bytes 36868
